TPU v7x, 512 devices: a whole 4x8x8 slice. The times are simulated.
512 devices in a mesh: blk: 64 (over z, y_hi, x), col: 8 (over y_lo, core).
Axes of the slice: x: 4, y: 8 (y_hi: 2, y_lo: 4; y = y_hi * 4 + y_lo), z: 8, core: 2. Of those that a mesh axis runs over, the one named last changes fastest.
Arguments:
- queries: bfloat16 [512, 16384], P('blk', 'col'), may hold values from -6 to 6
- factor: bfloat16 [16384, 1024], P('col', 'blk'), may hold values from -0.046875 to 0.046875
- eigenvalues: float32 [1024], replicated, may hold values from 0.05 to 20
- damping: float32 [1], replicated, may hold values from 0.5 to 2
- train_rows: bfloat16 [65536, 16384], P('blk', 'col'), may hold values from -0.046875 to 0.046875
Outputs:
- scores: bfloat16 [512, 65536], P('col', 'blk')
All inputs are finite; a program needn't handle non-finite values.
Results may differ from a plain program's by a relative error of at most 0.0049.
Values may be sent and summed in bfloat16 or wider, within the bound.
No kernel may reach another device: no remote copies, remote signals or barrier semaphores. Data moves between devices by JAX's collectives and lax.ppermute only.
A program may use at most 64 MiB of HBM per device.

v0:
```python
import jax
import jax.numpy as jnp
from jax import lax
from jax.sharding import Mesh
from jax.sharding import PartitionSpec as P

BLK = ("blk_0", "blk_1", "blk_2")


def in_order(tiles, dim):
    shape = list(tiles.shape[1:])
    shape[dim] *= tiles.shape[0]
    return jnp.moveaxis(tiles, 0, dim).reshape(shape)


def stacked_from(shard, axes, turns):
    tiles = shard[None]
    for k in turns:
        tiles = lax.all_gather(tiles, axes[k], axis=0, tiled=True)
    carried = [lax.axis_size(axes[k]) for k in reversed(turns)]
    tiles = tiles.reshape(*carried, *shard.shape)
    turned = sorted(range(len(turns)), key=lambda place: turns[len(turns) - 1 - place])
    return tiles.transpose(*turned, *range(len(turns), tiles.ndim)).reshape(-1, *shard.shape)


def gather_axes(shard, axes, turns, dim):
    return in_order(stacked_from(shard, axes, turns), dim)


def from_everyone(shard, axis):
    length = lax.axis_size(axis)
    return lax.all_to_all(
        jnp.broadcast_to(shard[None], (length, *shard.shape)), axis, 0, 0, tiled=True
    )


def taken_together(shard, axis):
    return from_everyone(shard, axis).sum(axis=0)


def row_scores(block_rows, train_rows):
    return jnp.einsum("qk,nk->qn", block_rows, train_rows, preferred_element_type=jnp.float32)


def per_device(queries, factor, eigenvalues, damping, train_rows):
    damp_value = damping[0]
    weights = eigenvalues / (eigenvalues + damp_value)
    full_factor = gather_axes(factor, BLK, (1, 0, 2), 1)
    partial_value = jnp.dot(queries, full_factor, preferred_element_type=jnp.float32)
    coefficient = taken_together(partial_value, "col")
    scaled = coefficient * weights[None, :]
    correction = jnp.dot(scaled, full_factor.astype(jnp.float32).T, precision=lax.Precision.HIGHEST)
    pre_own = ((queries.astype(jnp.float32) - correction) / damp_value).astype(jnp.bfloat16)
    partial_scores = row_scores(lax.all_gather(pre_own, BLK, axis=0, tiled=True), train_rows)
    scores = lax.psum_scatter(partial_scores, "col", scatter_dimension=0, tiled=True)
    return scores.astype(jnp.bfloat16)


def solution(mesh):
    split = Mesh(
        mesh.devices.reshape(8, 2, 4, mesh.shape["col"]), ("blk_0", "blk_1", "blk_2", "col")
    )
    in_specs = (P(BLK, "col"), P("col", BLK), P(), P(), P(BLK, "col"))
    out_specs = P("col", BLK)
    return jax.shard_map(
        per_device, mesh=split, in_specs=in_specs, out_specs=out_specs, check_vma=False
    )
```

profile of v0, /device:TPU:6, one launch (start us, length us, event | category | flops | bytes accessed | tf_op | source)
XLA Modules:
  0.0 330.9 jit_solution(12432319824471753628)
XLA Ops:
  6.5 0.0 all-gather.5.cloned.1.call-start
  6.5 9.7 %all-gather = bf16[4096,16]{0,1:T(8,128)(2,1)S(1)} all-gather(bf16[2048,16]{0,1:T(8,128)(2,1)} %param.6), channel_id=2, replica_groups=mesh['blk_0'=8,'blk_1'=2,'blk_2'=4,'col'=8] {'blk_1'}, dimensions={0}, use_global_device_ids=true | all-gather | bytes 196608 | tf_op jit(solution)/shard_map/all_gather | solution.py:19
  16.2 0.7 copy.17
  16.9 0.0 all-gather.5.cloned.1.call-update
  16.9 0.0 all-gather.7.cloned.1.call-start
  17.0 47.4 %all-gather.5.cloned.1.call-done = bf16[16,2048,16]{1,2,0:T(8,128)(2,1)} async-done(((bf16[2,2048,16]{1,2,0:T(8,128)(2,1)}), bf16[16,2048,16]{1,2,0:T(8,128)(2,1)}) %all-gather.5.cloned.1.call-update) | async-done | bytes 1048592 | tf_op jit(solution)/shard_map/all_gather | solution.py:19
  64.4 0.0 all-gather.7.cloned.1.call-update
  64.4 52.0 %all-gather.7.cloned.1.call-done = bf16[64,2048,16]{1,2,0:T(8,128)(2,1)} async-done(((bf16[16,2048,16]{1,2,0:T(8,128)(2,1)}), bf16[64,2048,16]{1,2,0:T(8,128)(2,1)}) %all-gather.7.cloned.1.call-update) | async-done | bytes 4194320 | tf_op jit(solution)/shard_map/all_gather | solution.py:19
  116.4 0.0 copy-start.1
  116.4 2.5 copy.14
  118.9 0.0 copy-start
  118.9 0.0 copy-start.2
  118.9 1.9 copy-done
  120.9 0.0 copy-done.1
  120.9 1.2 fusion.4
  122.1 0.7 broadcast_in_dim.5
  122.8 4.8 %all-to-all-start = ((f32[8,8,1024]{2,1,0:T(8,128)}), f32[8,8,1024]{2,1,0:T(8,128)S(1)}, u32[]{:S(2)}, u32[]{:S(2)}) async-start(f32[8,8,1024]{2,1,0:T(8,128)} %broadcast_in_dim.5), calls=%async_computation | async-start | bytes 524288 | tf_op jit(solution)/shard_map/all_to_all | solution.py:32
  127.6 0.0 all-gather.9.cloned.1.call-start
  128.3 0.0 copy-done.2
  128.4 9.0 %all-to-all-done = f32[8,8,1024]{2,1,0:T(8,128)S(1)} async-done(((f32[8,8,1024]{2,1,0:T(8,128)}), f32[8,8,1024]{2,1,0:T(8,128)S(1)}, u32[]{:S(2)}, u32[]{:S(2)}) %all-to-all-start) | async-done | bytes 262176 | tf_op jit(solution)/shard_map/all_to_all | solution.py:32
  137.4 4.5 %fusion.1 = bf16[8,2048]{1,0:T(8,128)(2,1)} fusion(bf16[2048,1024]{0,1:T(8,128)(2,1)} %bitcast.21, bf16[8,2048]{1,0:T(8,128)(2,1)S(1)} %copy-done.1, f32[]{:T(128)} %bitcast.19, f32[8,1024]{1,0:T(8,128)S(1)} %reduce_sum.9, f32[1024]{0:T(1024)S(1)} %add_divide_fusion), kind=kOutput, calls=%fused_computation.2 | convolution fusion | flops 201400320 | bytes 4296708 | tf_op jit(solution)/shard_map/dot_general | solution.py:52
  142.0 0.0 all-gather.9.cloned.1.call-update
  142.0 0.0 reduce-scatter.2.cloned.1.call-start
  142.0 134.0 %all-gather.9.cloned.1.call-done = bf16[512,2048]{1,0:T(8,128)(2,1)} async-done(((bf16[8,2048]{1,0:T(8,128)(2,1)}), bf16[512,2048]{1,0:T(8,128)(2,1)}) %all-gather.9.cloned.1.call-update) | async-done | bytes 2097168 | tf_op jit(solution)/shard_map/all_gather | solution.py:54
  276.1 6.5 %fusion.5 = f32[512,1024]{1,0:T(8,128)} fusion(bf16[512,2048]{1,0:T(8,128)(2,1)} %all-gather.9.cloned.1.call-done, bf16[1024,2048]{1,0:T(8,128)(2,1)} %param.9), kind=kOutput, calls=%fused_computation.8 | convolution fusion | flops 2147483648 | bytes 8388608 | tf_op jit(solution)/shard_map/qk,nk->qn/dot_general | solution.py:42
  282.6 0.0 reduce-scatter.2.cloned.1.call-update
  282.6 40.1 %reduce-scatter.2.cloned.1.call-done = f32[64,1024]{1,0:T(8,128)} async-done(((f32[512,1024]{1,0:T(8,128)}), f32[64,1024]{1,0:T(8,128)}) %reduce-scatter.2.cloned.1.call-update) | async-done | bytes 262160 | tf_op jit(solution)/shard_map/reduce_scatter | solution.py:55
  322.7 1.6 convert_element_type.12
  (2 shorter events, 0.0 us)
Async XLA Ops:
  6.5 57.8 %all-gather.5.cloned.1.call-start = ((), (), s32[]{:S(2)}) async-start(), calls=%async_computation.2 | async-start | bytes 1179648 | tf_op jit(solution)/shard_map/all_gather | solution.py:19
  16.9 99.5 %all-gather.7.cloned.1.call-start = ((), (), s32[]{:S(2)}) async-start(), calls=%async_computation.3 | async-start | bytes 5242880 | tf_op jit(solution)/shard_map/all_gather | solution.py:19
  116.4 4.5 %copy-start.1 = (bf16[8,2048]{1,0:T(8,128)(2,1)S(1)}, bf16[8,2048]{1,0:T(8,128)(2,1)}, u32[]{:S(2)}) copy-start(bf16[8,2048]{1,0:T(8,128)(2,1)} %param.5) | copy-start | bytes 98308
  118.9 2.0 copy-start
  118.9 9.4 %copy-start.2 = (f32[1024]{0:T(1024)S(1)}, f32[1024]{0:T(1024)}, u32[]{:S(2)}) copy-start(f32[1024]{0:T(1024)} %param.7) | copy-start | bytes 12292
  122.8 14.6 %all-to-all-start = ((f32[8,8,1024]{2,1,0:T(8,128)}), f32[8,8,1024]{2,1,0:T(8,128)S(1)}, u32[]{:S(2)}, u32[]{:S(2)}) async-start(f32[8,8,1024]{2,1,0:T(8,128)} %broadcast_in_dim.5), calls=%async_computation | async-start | bytes 524288 | tf_op jit(solution)/shard_map/all_to_all | solution.py:32
  127.6 148.4 %all-gather.9.cloned.1.call-start = ((), (), s32[]{:S(2)}) async-start(), calls=%async_computation.4 | async-start | bytes 2129920 | tf_op jit(solution)/shard_map/all_gather | solution.py:54
  142.0 180.7 %reduce-scatter.2.cloned.1.call-start = ((), (), s32[]{:S(2)}) async-start(), calls=%async_computation.5 | async-start | bytes 2359296 | tf_op jit(solution)/shard_map/reduce_scatter | solution.py:55
Sparse Core Ops, SparseCore 0:
  17.1 47.2 all-gather.4
  66.5 49.8 all-gather.6
  142.1 133.9 all-gather.8
  282.7 39.9 reduce-scatter.1
where the time goes:
time: 331 us
  waiting for transfers between devices  283 us (85%)
  between operations  13.8 us (4%)
  matrix products  12.2 us (4%)
  blocking collectives  9.7 us (3%)
  local copies, waits for them, and re-layouts  5.85 us (2%)
  starting transfers between devices  4.97 us (2%)
    all_gather x1, waiting for transfers between devices, per_device(): lax.all_gather(pre_own, BLK, axis=0, tiled=True)  134 us
    all_gather x2, waiting for transfers between devices, stacked_from(): tiles = lax.all_gather(tiles, axes[k], axis=0, tiled=True)  99.4 us
    reduce_scatter x1, waiting for transfers between devices, per_device(): lax.psum_scatter(partial_scores, 'col', scatter_dimension=0, tiled=True)  40.1 us
    all_gather x1, blocking collectives, stacked_from(): tiles = lax.all_gather(tiles, axes[k], axis=0, tiled=True)  9.7 us
    all_to_all x1, waiting for transfers between devices, from_everyone(): lax.all_to_all(jnp.broadcast_to(shard[None], (length, *shard.shape)), axi...  9.03 us
  transfers between devices with their start and end apart: 5, of which 5 were waited for; matrix products, arithmetic and copies ran while one was open for 0% of the time, Pallas kernels for 0%

commit v1 on v0

--- a/solution.py
+++ b/solution.py
@@ -51,7 +51,12 @@
     scaled = coefficient * weights[None, :]
     correction = jnp.dot(scaled, full_factor.astype(jnp.float32).T, precision=lax.Precision.HIGHEST)
     pre_own = ((queries.astype(jnp.float32) - correction) / damp_value).astype(jnp.bfloat16)
-    partial_scores = row_scores(lax.all_gather(pre_own, BLK, axis=0, tiled=True), train_rows)
+    partial_scores = row_scores(
+        jnp.concatenate(
+            lax.all_to_all(jnp.stack([pre_own] * lax.axis_size(BLK)), BLK, 0, 0), axis=0
+        ),
+        train_rows,
+    )
     scores = lax.psum_scatter(partial_scores, "col", scatter_dimension=0, tiled=True)
     return scores.astype(jnp.bfloat16)
 

time: 331 us -> 261 us (0.79)
  waiting for transfers between devices: 283 us -> 147 us
  blocking collectives: 9.7 us -> 78 us
  matrix products: 12.2 us -> 8.81 us
    all_gather x1 -> x0, waiting for transfers between devices: 134 us -> none  [per_device(): lax.all_gather(pre_own, BLK, axis=0, tiled=True)]
    all_to_all x0 -> x1, blocking collectives: none -> 68.3 us  [per_device(): lax.all_to_all(jnp.stack([pre_own] * lax.axis_size(BLK)), BLK, 0, 0)]
  transfers between devices with their start and end apart: 5 -> 4, of which waited for: 5 -> 4; matrix products, arithmetic and copies ran while one was open for 0% -> 0% of each run, Pallas kernels for 0% -> 0%
where the time goes in v1:
time: 261 us; the launch traced here: 260 us
  waiting for transfers between devices  147 us (56%)
  blocking collectives  78 us (30%)
  between operations  13.8 us (5%)
  matrix products  8.81 us (3%)
  local copies, waits for them, and re-layouts  6.09 us (2%)
  starting transfers between devices  4.92 us (2%)
    all_gather x2, waiting for transfers between devices, stacked_from(): tiles = lax.all_gather(tiles, axes[k], axis=0, tiled=True)  99.4 us
    all_to_all x1, blocking collectives, per_device(): lax.all_to_all(jnp.stack([pre_own] * lax.axis_size(BLK)), BLK, 0, 0)  68.3 us
    reduce_scatter x1, waiting for transfers between devices, per_device(): lax.psum_scatter(partial_scores, 'col', scatter_dimension=0, tiled=True)  38.4 us
    all_gather x1, blocking collectives, stacked_from(): tiles = lax.all_gather(tiles, axes[k], axis=0, tiled=True)  9.7 us
    all_to_all x1, waiting for transfers between devices, from_everyone(): lax.all_to_all(jnp.broadcast_to(shard[None], (length, *shard.shape)), axi...  9.03 us
  transfers between devices with their start and end apart: 4, of which 4 were waited for; matrix products, arithmetic and copies ran while one was open for 0% of the time, Pallas kernels for 0%

profile of v1, /device:TPU:6, one launch (start us, length us, event | category | flops | bytes accessed | tf_op | source)
XLA Modules:
  0.0 260.2 jit_solution(1611831401315342287)
XLA Ops:
  6.5 0.0 all-gather.4.cloned.1.call-start
  6.5 9.7 %all-gather = bf16[4096,16]{0,1:T(8,128)(2,1)S(1)} all-gather(bf16[2048,16]{0,1:T(8,128)(2,1)} %param.6), channel_id=2, replica_groups=mesh['blk_0'=8,'blk_1'=2,'blk_2'=4,'col'=8] {'blk_1'}, dimensions={0}, use_global_device_ids=true | all-gather | bytes 196608 | tf_op jit(solution)/shard_map/all_gather | solution.py:19
  16.2 0.7 copy.17
  16.9 0.0 all-gather.4.cloned.1.call-update
  16.9 0.0 all-gather.6.cloned.1.call-start
  17.0 47.4 %all-gather.4.cloned.1.call-done = bf16[16,2048,16]{1,2,0:T(8,128)(2,1)} async-done(((bf16[2,2048,16]{1,2,0:T(8,128)(2,1)}), bf16[16,2048,16]{1,2,0:T(8,128)(2,1)}) %all-gather.4.cloned.1.call-update) | async-done | bytes 1048592 | tf_op jit(solution)/shard_map/all_gather | solution.py:19
  64.4 0.0 all-gather.6.cloned.1.call-update
  64.4 52.0 %all-gather.6.cloned.1.call-done = bf16[64,2048,16]{1,2,0:T(8,128)(2,1)} async-done(((bf16[16,2048,16]{1,2,0:T(8,128)(2,1)}), bf16[64,2048,16]{1,2,0:T(8,128)(2,1)}) %all-gather.6.cloned.1.call-update) | async-done | bytes 4194320 | tf_op jit(solution)/shard_map/all_gather | solution.py:19
  116.4 0.0 copy-start.1
  116.4 2.5 copy.14
  118.9 0.0 copy-start
  118.9 0.0 copy-start.2
  118.9 1.9 copy-done
  120.9 0.0 copy-done.1
  120.9 1.2 fusion.6
  122.1 0.7 broadcast_in_dim.5
  122.8 4.8 %all-to-all-start = ((f32[8,8,1024]{2,1,0:T(8,128)}), f32[8,8,1024]{2,1,0:T(8,128)S(1)}, u32[]{:S(2)}, u32[]{:S(2)}) async-start(f32[8,8,1024]{2,1,0:T(8,128)} %broadcast_in_dim.5), calls=%async_computation | async-start | bytes 524288 | tf_op jit(solution)/shard_map/all_to_all | solution.py:32
  127.6 0.0 reduce-scatter.2.cloned.1.call-start
  128.3 0.0 copy-done.2
  128.3 9.0 %all-to-all-done = f32[8,8,1024]{2,1,0:T(8,128)S(1)} async-done(((f32[8,8,1024]{2,1,0:T(8,128)}), f32[8,8,1024]{2,1,0:T(8,128)S(1)}, u32[]{:S(2)}, u32[]{:S(2)}) %all-to-all-start) | async-done | bytes 262176 | tf_op jit(solution)/shard_map/all_to_all | solution.py:32
  137.4 3.9 %fusion.1 = bf16[8,2048]{1,0:T(8,128)(2,1)S(1)} fusion(bf16[2048,1024]{0,1:T(8,128)(2,1)} %bitcast.23, bf16[8,2048]{1,0:T(8,128)(2,1)S(1)} %copy-done.1, f32[]{:T(128)} %bitcast.21, f32[8,1024]{1,0:T(8,128)S(1)} %reduce_sum.9, f32[1024]{0:T(1024)S(1)} %add_divide_fusion), kind=kOutput, calls=%fused_computation.2 | convolution fusion | flops 201400320 | bytes 4296708 | tf_op jit(solution)/shard_map/dot_general | solution.py:52
  141.3 0.0 copy-start.3
  141.3 0.2 stack.2
  141.6 68.3 %all_to_all.10 = bf16[64,8,2048]{2,1,0:T(8,128)(2,1)S(1)} all-to-all(bf16[64,8,2048]{2,1,0:T(8,128)(2,1)S(1)} %stack.2), channel_id=1, replica_groups=mesh['blk_0'=8,'blk_1'=2,'blk_2'=4,'col'=8] {'blk_0','blk_1','blk_2'}, dimensions={0} | all-to-all | bytes 4194304 | tf_op jit(solution)/shard_map/all_to_all | solution.py:56
  209.9 0.0 copy-done.3
  209.9 3.7 %fusion.2 = f32[512,1024]{1,0:T(8,128)} fusion(bf16[1024,2048]{1,0:T(8,128)(2,1)S(1)} %copy-done.3, bf16[64,8,2048]{2,1,0:T(8,128)(2,1)S(1)} %all_to_all.10), kind=kOutput, calls=%fused_computation.3 | convolution fusion | flops 2147483648 | bytes 8388608 | tf_op jit(solution)/shard_map/qk,nk->qn/dot_general | solution.py:42
  213.6 0.0 reduce-scatter.2.cloned.1.call-update
  213.6 38.4 %reduce-scatter.2.cloned.1.call-done = f32[64,1024]{1,0:T(8,128)} async-done(((f32[512,1024]{1,0:T(8,128)}), f32[64,1024]{1,0:T(8,128)}) %reduce-scatter.2.cloned.1.call-update) | async-done | bytes 262160 | tf_op jit(solution)/shard_map/reduce_scatter | solution.py:60
  252.0 1.6 convert_element_type.12
  (2 shorter events, 0.0 us)
Async XLA Ops:
  6.5 57.8 %all-gather.4.cloned.1.call-start = ((), (), s32[]{:S(2)}) async-start(), calls=%async_computation.3 | async-start | bytes 1179648 | tf_op jit(solution)/shard_map/all_gather | solution.py:19
  16.9 99.5 %all-gather.6.cloned.1.call-start = ((), (), s32[]{:S(2)}) async-start(), calls=%async_computation.4 | async-start | bytes 5242880 | tf_op jit(solution)/shard_map/all_gather | solution.py:19
  116.4 4.5 %copy-start.1 = (bf16[8,2048]{1,0:T(8,128)(2,1)S(1)}, bf16[8,2048]{1,0:T(8,128)(2,1)}, u32[]{:S(2)}) copy-start(bf16[8,2048]{1,0:T(8,128)(2,1)} %param.5) | copy-start | bytes 98308
  118.9 1.9 copy-start
  118.9 9.4 %copy-start.2 = (f32[1024]{0:T(1024)S(1)}, f32[1024]{0:T(1024)}, u32[]{:S(2)}) copy-start(f32[1024]{0:T(1024)} %param.7) | copy-start | bytes 12292
  122.8 14.6 %all-to-all-start = ((f32[8,8,1024]{2,1,0:T(8,128)}), f32[8,8,1024]{2,1,0:T(8,128)S(1)}, u32[]{:S(2)}, u32[]{:S(2)}) async-start(f32[8,8,1024]{2,1,0:T(8,128)} %broadcast_in_dim.5), calls=%async_computation | async-start | bytes 524288 | tf_op jit(solution)/shard_map/all_to_all | solution.py:32
  127.6 124.4 %reduce-scatter.2.cloned.1.call-start = ((), (), s32[]{:S(2)}) async-start(), calls=%async_computation.5 | async-start | bytes 2359296 | tf_op jit(solution)/shard_map/reduce_scatter | solution.py:60
  141.3 68.6 %copy-start.3 = (bf16[1024,2048]{1,0:T(8,128)(2,1)S(1)}, bf16[1024,2048]{1,0:T(8,128)(2,1)}, u32[]{:S(2)}) copy-start(bf16[1024,2048]{1,0:T(8,128)(2,1)} %param.9) | copy-start | bytes 12582916
Sparse Core Ops, SparseCore 0:
  17.1 47.2 all-gather.3
  66.5 49.8 all-gather.5
  213.7 38.2 reduce-scatter.1
